TPU v7x, 32 devices: a whole 2x2x4 slice. The times are simulated.
32 devices in a mesh: gx: 8 (over z, x), gy: 4 (over y, core).
Axes of the slice: x: 2, y: 2, z: 4, core: 2. Of those that a mesh axis runs over, the one named last changes fastest.
Arguments:
- krylov_block: float32 [16, 26, 64, 1024], P(None, None, 'gx', 'gy'), may hold values from -13 to 13
- prior_basis: float32 [24, 26, 64, 1024], P(None, None, 'gx', 'gy'), may hold values from -5.2 to 5.2
- flux_along: float32 [26, 26], replicated, may hold values from -1.25 to 1.25
- flux_across: float32 [26, 26], replicated, may hold values from -1.25 to 1.25
- collision: float32 [64, 1024], P('gx', 'gy'), may hold values from 1 to 10
- field_rates: float32 [26], replicated, may hold values from 0.5 to 2
- wall_table: float32 [4, 26], replicated, may hold values from 0.5 to 3
- wall_mask: int32 [64, 1024], P('gx', 'gy'), may hold values 0 or 1
- wall_type: int32 [64, 1024], P('gx', 'gy'), may hold values from 0 to 3
Outputs:
- new_block: float32 [16, 26, 64, 1024], P(None, None, 'gx', 'gy')
- projection: float32 [24, 16], replicated
- triangle: float32 [16, 16], replicated
All inputs are finite; a program needn't handle non-finite values. No bound on the sum of `wall_mask` on one device may be relied on, other than what follows from the above.
Results may differ from a plain program's by a relative error of at most 0.0003.
Values sent between devices are 32-bit elements; how exact they have to be, the bound alone decides.
A program may use at most 128 MiB of HBM per device.

v0:
```python
import functools

import jax
import jax.numpy as jnp
from jax import lax
from jax.experimental import pallas as pl
from jax.experimental.pallas import tpu as pltpu
from jax.sharding import PartitionSpec as P

damping = 0.0625
precise = lax.Precision.HIGHEST
f32, b16 = jnp.float32, jnp.bfloat16


def dot(a, b, precision=None):
    return lax.dot_general(
        a, b, (((1,), (0,)), ((), ())), precision=precision, preferred_element_type=f32
    )


def dot_t(a, b, precision=None):
    return lax.dot_general(
        a, b, (((1,), (1,)), ((), ())), precision=precision, preferred_element_type=f32
    )


def iota(shape, dim):
    return lax.broadcasted_iota(jnp.int32, shape, dim)


def pieces(a):
    high = a.astype(b16).astype(f32)
    rest = a - high
    mid = rest.astype(b16).astype(f32)
    return high, mid, (rest - mid).astype(b16).astype(f32)


def factor(a):
    size = a.shape[0]
    row, col = iota(a.shape, 0), iota(a.shape, 1)
    row1 = iota((size, 1), 0)
    inv = jnp.where(row == col, 1.0, 0.0).astype(f32)
    for j in range(size):
        scale = jnp.where(row1 > j, a[:, j : j + 1] / a[j : j + 1, j : j + 1], 0.0)
        inv = inv - scale * inv[j : j + 1, :]
        a = a - scale * a[j : j + 1, :]
    diag = jnp.sum(jnp.where(row == col, a, 0.0), axis=1, keepdims=True)
    root = 1.0 / jnp.sqrt(diag)
    return jnp.where(col >= row, a * root, 0.0), inv * root


def selector(count, width, start, levels):
    row, col = iota((count, width), 0), iota((count, width), 1)
    hit = col == row + start
    for level in range(1, levels):
        hit = hit | (col == row + (start + level * count))
    return jnp.where(hit, 1.0, 0.0).astype(f32)


def spread(parts, width):
    blocks = []
    for level in range(3):
        total = None
        for weights, start in parts:
            term = dot(
                pieces(weights)[level].astype(b16),
                selector(weights.shape[1], width, start, 3 - level).astype(b16),
            )
            total = term if total is None else total + term
        blocks.append(total)
    return jnp.concatenate(blocks, axis=0).astype(b16)


def fold_rows(a, count):
    return a[:count] + a[count : 2 * count] + a[2 * count : 3 * count]


def kernel(
    dims, inv_cells,
    kry, pri, along, across, coll, rates, table, wmask, wtype,
    out, proj_out, tri_out,
    kv, pv, vals, left, right, app, grad, kron_h, kron_l, stack, ortho, tile,
    y1, x1, y2, x2, local_sem, halo_send, halo_recv,
    y1s, y1r, x1s, x1r, y2s, y2r, x2s, x2r,
):
    m, k, nf, nx, ny, types = dims
    rows = nf * m
    block = 3 * m
    width = stack.shape[1]
    gx, gy = lax.axis_index("gx"), lax.axis_index("gy")
    px, py = lax.axis_size("gx"), lax.axis_size("gy")
    MESH = pl.DeviceIdType.MESH

    halves = ny // 128
    load_k = pltpu.make_async_copy(kry, kv, local_sem.at[0])
    load_p = pltpu.make_async_copy(pri, pv, local_sem.at[1])
    load_k.start()
    load_p.start()

    def lines(f, x, h, count):
        return pl.ds((f * halves + h) * nx + x, count, stride=nf * halves * nx)

    barrier = pltpu.get_barrier_semaphore()
    for axis, me, n in (("gy", gy, py), ("gx", gx, px)):
        for off in range(1, n):
            pl.semaphore_signal(
                barrier, inc=1, device_id={axis: lax.rem(me + off, n)}, device_id_type=MESH
            )
    pl.semaphore_wait(barrier, px + py - 2)

    load_k.wait()

    def to_rows(x):
        def body(f, carry):
            at = pl.multiple_of(f * m, m)
            for h in range(halves):
                lanes = pl.ds(h * 128, 128)
                vals[x + 2, pl.ds(at, m), lanes] = kv[lines(f, x, h, m), :]
            return carry

        lax.fori_loop(0, nf, body, 0, unroll=2)

    def remote(src, dst, index, where):
        return pltpu.make_async_remote_copy(
            src_ref=src, dst_ref=dst, send_sem=halo_send.at[index], recv_sem=halo_recv.at[index],
            device_id=where, device_id_type=MESH,
        )

    send_up = remote(vals.at[pl.ds(nx, 2)], vals.at[pl.ds(0, 2)], 0, {"gx": lax.rem(gx + 1, px)})
    send_down = remote(
        vals.at[pl.ds(2, 2)], vals.at[pl.ds(nx + 2, 2)], 1, {"gx": lax.rem(gx + px - 1, px)}
    )
    send_right = remote(
        vals.at[pl.ds(2, nx), :, pl.ds(ny - 128, 128)], left, 2, {"gy": lax.rem(gy + 1, py)}
    )
    send_left = remote(
        vals.at[pl.ds(2, nx), :, pl.ds(0, 128)], right, 3, {"gy": lax.rem(gy + py - 1, py)}
    )

    for x in (nx - 2, nx - 1):
        to_rows(x)
    pl.when(gx < px - 1)(send_up.start)
    for x in (0, 1):
        to_rows(x)
    pl.when(gx > 0)(send_down.start)

    def to_rows_inner(x, carry):
        to_rows(x)
        return carry

    lax.fori_loop(2, nx - 2, to_rows_inner, 0)
    pl.when(gy < py - 1)(send_right.start)
    pl.when(gy > 0)(send_left.start)

    @pl.when(gx == 0)
    def _():
        vals[0:2] = jnp.zeros((2, rows, ny), f32)

    @pl.when(gx == px - 1)
    def _():
        vals[nx + 2 : nx + 4] = jnp.zeros((2, rows, ny), f32)

    @pl.when(gy == 0)
    def _():
        left[...] = jnp.zeros(left.shape, f32)

    @pl.when(gy == py - 1)
    def _():
        right[...] = jnp.zeros(right.shape, f32)

    pick = jnp.where(iota((rows, nf), 0) // m == iota((rows, nf), 1), 1.0, 0.0).astype(f32)
    same = (iota((rows, rows), 0) % m) == (iota((rows, rows), 1) % m)
    for index, flux in enumerate((along, across)):
        full = jnp.where(same, dot_t(dot(pick, flux[...], precise), pick, precise), 0.0)
        high = full.astype(b16)
        kron_h[index] = high
        kron_l[index] = (full - high.astype(f32)).astype(b16)

    load_p.wait()

    def prior_step(i, total):
        x, f = i // nf, i % nf
        cols = []
        for h in range(halves):
            cols.append(pv[lines(f, x, h, k), :])
        p = jnp.concatenate(cols, axis=1)
        parts = list(pieces(p))
        pad = width - block - 3 * k
        if pad:
            parts.append(jnp.zeros((pad, ny), f32))
        both = jnp.concatenate(parts, axis=0).astype(b16)
        stack[i, block:width, :] = both
        return total + dot_t(both, both)

    basis = lax.fori_loop(
        0, nf * nx, prior_step, jnp.zeros((width - block, width - block), f32), unroll=2
    )
    tile[...] = jnp.zeros(tile.shape, f32)
    tile[m : m + k, 0 : width - block] = fold_rows(basis, k) * inv_cells

    def operate(x):
        row_c = jnp.broadcast_to(coll[pl.ds(x, 1), :], (m, ny))
        mask = wmask[pl.ds(x, 1), :].astype(f32)
        kind = wtype[pl.ds(x, 1), :]
        gains = [
            jnp.broadcast_to(jnp.where(kind == t, mask, 0.0), (m, ny)) for t in range(types)
        ]

        def body(f, carry):
            at = pl.ds(pl.multiple_of(f * m, m), m)
            v = vals[x + 2, at, :]
            coeff = row_c * rates[f]
            for t in range(types):
                coeff = coeff + gains[t] * table[t, f]
            b2, b1, a1, a2 = (vals[x + s, at, :] for s in (0, 1, 3, 4))
            ext = jnp.concatenate([left[x, at, :], v, right[x, at, :]], axis=1)
            span = ny + 256
            c2, c1, d1, d2 = (
                pltpu.roll(ext, s % span, 1)[:, 128 : 128 + ny] for s in (2, 1, -1, -2)
            )
            fourth = b2 - 4.0 * b1 + 6.0 * v - 4.0 * a1 + a2
            fourth = fourth + c2 - 4.0 * c1 + 6.0 * v - 4.0 * d1 + d2
            app[at, :] = coeff * v + damping * fourth
            for index, g in enumerate((0.5 * (a1 - b1), 0.5 * (d1 - c1))):
                high = g.astype(b16)
                grad[index, 0, at, :] = high
                grad[index, 1, at, :] = (g - high.astype(f32)).astype(b16)
            return carry

        lax.fori_loop(0, nf, body, 0, unroll=2)
        for index in range(2):
            high, low = grad[index, 0], grad[index, 1]
            app[...] += (
                dot(kron_h[index], high) + dot(kron_h[index], low) + dot(kron_l[index], high)
            )

    def gram(x, total):
        def body(f, total):
            a = app[pl.ds(pl.multiple_of(f * m, m), m), :]
            both = jnp.concatenate(pieces(a), axis=0).astype(b16)
            i = x * nf + f
            stack[i, 0:block, :] = both
            return total + dot_t(both, stack[i])

        return lax.fori_loop(0, nf, body, total, unroll=2)

    def row_step(x, total):
        operate(x)
        return gram(x, total)

    pl.when(gy > 0)(send_right.wait_recv)
    pl.when(gy < py - 1)(send_left.wait_recv)
    total = jnp.zeros((block, width), f32)
    total = lax.fori_loop(2, nx - 2, row_step, total)
    pl.when(gx > 0)(send_up.wait_recv)
    pl.when(gx < px - 1)(send_down.wait_recv)
    total = lax.fori_loop(
        0, 4, lambda j, t: row_step(j + (j // 2) * (nx - 4), t), total
    )

    def all_reduce(value, bufs):
        for axis, me, n, buf, ss, rs in bufs:
            buf[me] = value
            copies = []
            for off in range(1, n):
                copy = pltpu.make_async_remote_copy(
                    src_ref=buf.at[me], dst_ref=buf.at[me],
                    send_sem=ss.at[off - 1], recv_sem=rs.at[off - 1],
                    device_id={axis: lax.rem(me + off, n)}, device_id_type=MESH,
                )
                copy.start()
                copies.append(copy)
            for copy in copies:
                copy.wait()
            value = buf[0]
            for j in range(1, n):
                value = value + buf[j]
        return value

    tile[0:m, :] = fold_rows(total, m) * inv_cells
    sums = all_reduce(
        tile[...], (("gy", gy, py, y1, y1s, y1r), ("gx", gx, px, x1, x1s, x1r))
    )
    top = sums[0:m]
    own = dot_t(top, selector(m, width, 0, 3), precise)
    first = dot_t(top, selector(k, width, block, 3), precise)
    basis_gram = dot_t(sums[m : m + k], selector(k, width, 0, 3), precise)
    proj = first + (first - dot(first, basis_gram, precise))
    cross = dot_t(proj, first, precise)
    cross_t = dot_t(first, proj, precise)
    square = dot_t(dot(proj, basis_gram, precise), proj, precise)
    upper_one, inv_one = factor(own - cross - cross_t + square)
    eye = jnp.where(iota((k, k), 0) == iota((k, k), 1), 1.0, 0.0).astype(f32)
    proj_out[...] = dot_t(eye, proj, precise)

    mixing = spread(((inv_one, 0), (-dot(inv_one, proj, precise), block)), width)

    def mix_step(i, total):
        q = fold_rows(dot(mixing, stack[i]), m)
        both = jnp.concatenate(pieces(q), axis=0).astype(b16)
        ortho[i] = both
        return total + dot_t(both, both)

    second = lax.fori_loop(0, nf * nx, mix_step, jnp.zeros((block, block), f32), unroll=4)
    tile[0:m, 0:block] = fold_rows(second, m) * inv_cells
    tile[0:m, block:width] = jnp.zeros((m, width - block), f32)
    sums = all_reduce(
        tile[0:m, :], (("gy", gy, py, y2, y2s, y2r), ("gx", gx, px, x2, x2s, x2r))
    )
    upper_two, inv_two = factor(dot_t(sums, selector(m, width, 0, 3), precise))
    tri_out[...] = dot(upper_two, upper_one, precise)
    last = spread(((inv_two, 0),), block)

    def last_step(i, carry):
        x, f = i // nf, i % nf
        q = fold_rows(dot(last, ortho[i]), m)
        for h in range(halves):
            out[lines(f, x, h, m), :] = q[:, h * 128 : (h + 1) * 128]
        return carry

    lax.fori_loop(0, nf * nx, last_step, 0, unroll=4)

    pl.when(gx < px - 1)(send_up.wait_send)
    pl.when(gx > 0)(send_down.wait_send)
    pl.when(gy < py - 1)(send_right.wait_send)
    pl.when(gy > 0)(send_left.wait_send)


def in_tiles(a):
    n, f, x, y = a.shape
    return a.reshape(n, f, x, y // 128, 128).transpose(0, 1, 3, 2, 4).reshape(-1, 128)


def on_device(
    krylov_block, prior_basis, flux_along, flux_across, collision, field_rates,
    wall_table, wall_mask, wall_type,
):
    m, nf, nx, ny = krylov_block.shape
    k, types = prior_basis.shape[0], wall_table.shape[0]
    px, py = lax.axis_size("gx"), lax.axis_size("gy")
    inv_cells = 1.0 / (nf * nx * px * ny * py)
    block = 3 * m
    width = block + -(-3 * k // 16) * 16
    rows, halves = nf * m, ny // 128
    hbm = pl.BlockSpec(memory_space=pl.ANY)
    vmem = pl.BlockSpec(memory_space=pltpu.VMEM)
    smem = pl.BlockSpec(memory_space=pltpu.SMEM)
    sems = pltpu.SemaphoreType.DMA
    new, proj, tri = pl.pallas_call(
        functools.partial(kernel, (m, k, nf, nx, ny, types), inv_cells),
        out_shape=(
            jax.ShapeDtypeStruct((halves * m * nf * nx, 128), f32),
            jax.ShapeDtypeStruct((k, m), f32),
            jax.ShapeDtypeStruct((m, m), f32),
        ),
        in_specs=[hbm, hbm, vmem, vmem, vmem, smem, smem, vmem, vmem],
        out_specs=(vmem, vmem, vmem),
        scratch_shapes=[
            pltpu.VMEM((halves * m * nf * nx, 128), f32),
            pltpu.VMEM((halves * k * nf * nx, 128), f32),
            pltpu.VMEM((nx + 4, rows, ny), f32),
            pltpu.VMEM((nx, rows, 128), f32),
            pltpu.VMEM((nx, rows, 128), f32),
            pltpu.VMEM((rows, ny), f32),
            pltpu.VMEM((2, 2, rows, ny), b16),
            pltpu.VMEM((2, rows, rows), b16),
            pltpu.VMEM((2, rows, rows), b16),
            pltpu.VMEM((nf * nx, width, ny), b16),
            pltpu.VMEM((nf * nx, block, ny), b16),
            pltpu.VMEM((m + k, width), f32),
            pltpu.VMEM((py, m + k, width), f32),
            pltpu.VMEM((px, m + k, width), f32),
            pltpu.VMEM((py, m, width), f32),
            pltpu.VMEM((px, m, width), f32),
            sems((2,)), sems((4,)), sems((4,)),
            sems((py - 1,)), sems((py - 1,)), sems((px - 1,)), sems((px - 1,)),
            sems((py - 1,)), sems((py - 1,)), sems((px - 1,)), sems((px - 1,)),
        ],
        compiler_params=pltpu.CompilerParams(
            collective_id=0, has_side_effects=True, vmem_limit_bytes=60 * 1024 * 1024
        ),
    )(
        in_tiles(krylov_block), in_tiles(prior_basis), flux_along, flux_across, collision,
        field_rates, wall_table, wall_mask, wall_type,
    )
    new = new.reshape(m, nf, halves, nx, 128).transpose(0, 1, 3, 2, 4).reshape(m, nf, nx, ny)
    return (new, proj, tri)


def solution(mesh):
    placed = (
        P(None, None, "gx", "gy"), P(None, None, "gx", "gy"), P(), P(), P("gx", "gy"),
        P(), P(), P("gx", "gy"), P("gx", "gy"),
    )
    return jax.shard_map(
        on_device,
        mesh=mesh,
        in_specs=placed,
        out_specs=(P(None, None, "gx", "gy"), P(), P()),
        check_vma=False,
    )
```

profile of v0, /device:TPU:0, one launch (start us, length us, event | category | flops | bytes accessed | tf_op | source)
XLA Modules:
  0.0 129.2 jit_solution(2220145103801309960)
XLA Ops:
  0.6 122.6 %shard_map.112 = (f32[6656,128]{1,0:T(8,128)}, f32[24,16]{1,0:T(8,128)}, f32[16,16]{1,0:T(8,128)}) custom-call(f32[6656,128]{1,0:T(8,128)} %bitcast.16, f32[9984,128]{1,0:T(8,128)} %bitcast.15, f32[26,26]{1,0:T(8,128)} %along.1, f32[26,26]{1,0:T(8,128)} %across.1, f32[8,256]{1,0:T(8,128)} %coll.1, f32[26]{0:T(128)} %rates.1, f32[4,26]{1,0:T(4,128)} %table.1, ...), custom_call_target="tpu_custom_call" | custom-call | tf_op jit(solution)/shard_map/pallas_call | solution.py:349
  123.2 1.4 %copy.12 = f32[24,16]{0,1:T(8,128)} copy(f32[24,16]{1,0:T(8,128)} %get-tuple-element.10) | data formatting | bytes 3072
  124.6 0.0 copy-start
  124.6 4.0 %copy.15 = f32[16,26,8,256]{3,2,1,0:T(8,128)} copy(f32[16,26,8,256]{3,2,1,0:T(8,128)} %bitcast.17) | data formatting | bytes 6815744
  128.6 0.0 copy-done
  128.6 0.6 copy.16
Async XLA Ops:
  124.6 4.0 %copy-start = (f32[16,16]{1,0:T(8,128)S(1)}, f32[16,16]{1,0:T(8,128)}, u32[]{:S(2)}) copy-start(f32[16,16]{1,0:T(8,128)} %get-tuple-element.17) | copy-start | bytes 3076
where the time goes:
time: 129 us
  Pallas kernels  123 us (95%)
  local copies, waits for them, and re-layouts  5.97 us (5%)
    pallas_call x1, Pallas kernels, on_device(): pl.pallas_call(functools.partial(kernel, (m, k, nf, nx, ny, types), inv_c...  123 us
    unnamed x5, local copies, waits for them, and re-layouts  5.97 us

commit v1 on v0

--- a/solution.py
+++ b/solution.py
@@ -49,44 +49,42 @@
     return jnp.where(col >= row, a * root, 0.0), inv * root
 
 
-def selector(count, width, start, levels):
-    row, col = iota((count, width), 0), iota((count, width), 1)
-    hit = col == row + start
-    for level in range(1, levels):
-        hit = hit | (col == row + (start + level * count))
+def where01(hit):
     return jnp.where(hit, 1.0, 0.0).astype(f32)
 
 
-def spread(parts, width):
+def spread(parts, levels, groups, group_of):
     blocks = []
-    for level in range(3):
+    for level in range(levels):
         total = None
-        for weights, start in parts:
-            term = dot(
-                pieces(weights)[level].astype(b16),
-                selector(weights.shape[1], width, start, 3 - level).astype(b16),
-            )
+        for weights, pick in parts:
+            term = dot(pieces(weights)[level].astype(b16), pick(level).astype(b16))
             total = term if total is None else total + term
-        blocks.append(total)
+        for group in range(groups):
+            blocks.append(jnp.where(group_of == group, total, 0.0))
     return jnp.concatenate(blocks, axis=0).astype(b16)
 
 
 def fold_rows(a, count):
-    return a[:count] + a[count : 2 * count] + a[2 * count : 3 * count]
+    total = a[:count]
+    for start in range(count, a.shape[0], count):
+        total = total + a[start : start + count]
+    return total
 
 
 def kernel(
     dims, inv_cells,
     kry, pri, along, across, coll, rates, table, wmask, wtype,
     out, proj_out, tri_out,
-    kv, pv, vals, left, right, app, grad, kron_h, kron_l, stack, ortho, tile,
+    kv, pv, vals, left, right, low_x, high_x, app, grad, kron_h, kron_l, stack, ortho, tile,
     y1, x1, y2, x2, local_sem, halo_send, halo_recv,
     y1s, y1r, x1s, x1r, y2s, y2r, x2s, x2r,
 ):
     m, k, nf, nx, ny, types = dims
     rows = nf * m
-    block = 3 * m
-    width = stack.shape[1]
+    steps = nf * nx
+    own3 = 6 * m
+    pad_k = (stack.shape[1] - own3) // 2
     gx, gy = lax.axis_index("gx"), lax.axis_index("gy")
     px, py = lax.axis_size("gx"), lax.axis_size("gy")
     MESH = pl.DeviceIdType.MESH
@@ -126,9 +124,9 @@
             device_id=where, device_id_type=MESH,
         )
 
-    send_up = remote(vals.at[pl.ds(nx, 2)], vals.at[pl.ds(0, 2)], 0, {"gx": lax.rem(gx + 1, px)})
+    send_up = remote(vals.at[pl.ds(nx, 2)], low_x, 0, {"gx": lax.rem(gx + 1, px)})
     send_down = remote(
-        vals.at[pl.ds(2, 2)], vals.at[pl.ds(nx + 2, 2)], 1, {"gx": lax.rem(gx + px - 1, px)}
+        vals.at[pl.ds(2, 2)], high_x, 1, {"gx": lax.rem(gx + px - 1, px)}
     )
     send_right = remote(
         vals.at[pl.ds(2, nx), :, pl.ds(ny - 128, 128)], left, 2, {"gy": lax.rem(gy + 1, py)}
@@ -152,13 +150,8 @@
     pl.when(gy < py - 1)(send_right.start)
     pl.when(gy > 0)(send_left.start)
 
-    @pl.when(gx == 0)
-    def _():
-        vals[0:2] = jnp.zeros((2, rows, ny), f32)
-
-    @pl.when(gx == px - 1)
-    def _():
-        vals[nx + 2 : nx + 4] = jnp.zeros((2, rows, ny), f32)
+    vals[0:2] = jnp.zeros((2, rows, ny), f32)
+    vals[nx + 2 : nx + 4] = jnp.zeros((2, rows, ny), f32)
 
     @pl.when(gy == 0)
     def _():
@@ -178,27 +171,32 @@
 
     load_p.wait()
 
-    def prior_step(i, total):
-        x, f = i // nf, i % nf
-        cols = []
-        for h in range(halves):
-            cols.append(pv[lines(f, x, h, k), :])
-        p = jnp.concatenate(cols, axis=1)
-        parts = list(pieces(p))
-        pad = width - block - 3 * k
-        if pad:
-            parts.append(jnp.zeros((pad, ny), f32))
-        both = jnp.concatenate(parts, axis=0).astype(b16)
-        stack[i, block:width, :] = both
+    def prior_step(pair, total):
+        pairs = []
+        for half in range(2):
+            i = 2 * pair + half
+            x, f = i // nf, i % nf
+            p = jnp.concatenate([pv[lines(f, x, h, k), :] for h in range(halves)], axis=1)
+            parts = list(pieces(p))
+            if pad_k > 3 * k:
+                parts.append(jnp.zeros((pad_k - 3 * k, ny), f32))
+            both = jnp.concatenate(parts, axis=0).astype(b16)
+            start = own3 + half * pad_k
+            stack[pair, start : start + pad_k, :] = both
+            pairs.append(both[0 : 2 * k])
+        both = jnp.concatenate(pairs, axis=0)
         return total + dot_t(both, both)
 
     basis = lax.fori_loop(
-        0, nf * nx, prior_step, jnp.zeros((width - block, width - block), f32), unroll=2
-    )
+        0, steps // 2, prior_step, jnp.zeros((4 * k, 4 * k), f32), unroll=4
+    )
+    wide = (4 * k, 4 * k)
+    basis = jnp.where(iota(wide, 0) // (2 * k) == iota(wide, 1) // (2 * k), basis, 0.0)
+    pick_k = where01(iota((k, 4 * k), 1) % k == iota((k, 4 * k), 0))
     tile[...] = jnp.zeros(tile.shape, f32)
-    tile[m : m + k, 0 : width - block] = fold_rows(basis, k) * inv_cells
-
-    def operate(x):
+    tile[m : m + k, 0:k] = dot_t(fold_rows(basis, k), pick_k, precise) * inv_cells
+
+    def operate(x, carry_x):
         row_c = jnp.broadcast_to(coll[pl.ds(x, 1), :], (m, ny))
         mask = wmask[pl.ds(x, 1), :].astype(f32)
         kind = wtype[pl.ds(x, 1), :]
@@ -220,7 +218,7 @@
             )
             fourth = b2 - 4.0 * b1 + 6.0 * v - 4.0 * a1 + a2
             fourth = fourth + c2 - 4.0 * c1 + 6.0 * v - 4.0 * d1 + d2
-            app[at, :] = coeff * v + damping * fourth
+            app[x, at, :] = coeff * v + damping * fourth
             for index, g in enumerate((0.5 * (a1 - b1), 0.5 * (d1 - c1))):
                 high = g.astype(b16)
                 grad[index, 0, at, :] = high
@@ -230,33 +228,57 @@
         lax.fori_loop(0, nf, body, 0, unroll=2)
         for index in range(2):
             high, low = grad[index, 0], grad[index, 1]
-            app[...] += (
-                dot(kron_h[index], high) + dot(kron_h[index], low) + dot(kron_l[index], high)
-            )
+            app[x] += dot(kron_h[index], high) + dot(kron_h[index], low) + dot(kron_l[index], high)
+        return carry_x
 
     def gram(x, total):
-        def body(f, total):
-            a = app[pl.ds(pl.multiple_of(f * m, m), m), :]
+        def body(t, total):
+            a = app[x, pl.ds(pl.multiple_of(t * 2 * m, 2 * m), 2 * m), :]
             both = jnp.concatenate(pieces(a), axis=0).astype(b16)
-            i = x * nf + f
-            stack[i, 0:block, :] = both
-            return total + dot_t(both, stack[i])
-
-        return lax.fori_loop(0, nf, body, total, unroll=2)
-
-    def row_step(x, total):
-        operate(x)
-        return gram(x, total)
+            pair = x * (nf // 2) + t
+            stack[pair, 0:own3, :] = both
+            own = both[0 : 4 * m]
+            right_side = [own]
+            for half in range(2):
+                start = own3 + half * pad_k
+                right_side.append(stack[pair, start : start + 2 * k, :])
+            return total + dot_t(own, jnp.concatenate(right_side, axis=0))
+
+        return lax.fori_loop(0, nf // 2, body, total, unroll=nf // 2)
 
     pl.when(gy > 0)(send_right.wait_recv)
     pl.when(gy < py - 1)(send_left.wait_recv)
-    total = jnp.zeros((block, width), f32)
-    total = lax.fori_loop(2, nx - 2, row_step, total)
-    pl.when(gx > 0)(send_up.wait_recv)
-    pl.when(gx < px - 1)(send_down.wait_recv)
-    total = lax.fori_loop(
-        0, 4, lambda j, t: row_step(j + (j // 2) * (nx - 4), t), total
-    )
+    lax.fori_loop(0, nx, operate, 0)
+    total = jnp.zeros((4 * m, 4 * m + 4 * k), f32)
+    total = lax.fori_loop(2, nx - 2, gram, total)
+
+    def add_halo(near, far, x_near, x_far, sign):
+        def body(f, carry):
+            at = pl.ds(pl.multiple_of(f * m, m), m)
+            v = near[at, :]
+            app[x_near, at, :] += damping * (far[at, :] - 4.0 * v)
+            app[x_far, at, :] += damping * v
+            g = (0.5 * sign) * v
+            high = g.astype(b16)
+            grad[0, 0, at, :] = high
+            grad[0, 1, at, :] = (g - high.astype(f32)).astype(b16)
+            return carry
+
+        lax.fori_loop(0, nf, body, 0, unroll=2)
+        high, low = grad[0, 0], grad[0, 1]
+        app[x_near] += dot(kron_h[0], high) + dot(kron_h[0], low) + dot(kron_l[0], high)
+
+    @pl.when(gx > 0)
+    def _():
+        send_up.wait_recv()
+        add_halo(low_x.at[1], low_x.at[0], 0, 1, -1.0)
+
+    @pl.when(gx < px - 1)
+    def _():
+        send_down.wait_recv()
+        add_halo(high_x.at[0], high_x.at[1], nx - 1, nx - 2, 1.0)
+
+    total = lax.fori_loop(0, 4, lambda j, t: gram(j + (j // 2) * (nx - 4), t), total)
 
     def all_reduce(value, bufs):
         for axis, me, n, buf, ss, rs in bufs:
@@ -277,48 +299,89 @@
                 value = value + buf[j]
         return value
 
-    tile[0:m, :] = fold_rows(total, m) * inv_cells
+    total = fold_rows(total, 2 * m)
+    col = iota(total.shape, 1)
+    group = jnp.where(col < 4 * m, (col // m) % 2, (col - 4 * m) // (2 * k))
+    total = fold_rows(jnp.where(group == iota(total.shape, 0) // m, total, 0.0), m)
+    shape = (4 * m + 4 * k, tile.shape[1])
+    row, col = iota(shape, 0), iota(shape, 1)
+    fold = where01(col == jnp.where(row < 4 * m, row % m, m + (row - 4 * m) % k))
+    tile[0:m, :] = dot(total, fold, precise) * inv_cells
     sums = all_reduce(
         tile[...], (("gy", gy, py, y1, y1s, y1r), ("gx", gx, px, x1, x1s, x1r))
     )
     top = sums[0:m]
-    own = dot_t(top, selector(m, width, 0, 3), precise)
-    first = dot_t(top, selector(k, width, block, 3), precise)
-    basis_gram = dot_t(sums[m : m + k], selector(k, width, 0, 3), precise)
+    own, first = top[:, 0:m], top[:, m : m + k]
+    basis_gram = sums[m : m + k, 0:k]
     proj = first + (first - dot(first, basis_gram, precise))
     cross = dot_t(proj, first, precise)
     cross_t = dot_t(first, proj, precise)
     square = dot_t(dot(proj, basis_gram, precise), proj, precise)
     upper_one, inv_one = factor(own - cross - cross_t + square)
-    eye = jnp.where(iota((k, k), 0) == iota((k, k), 1), 1.0, 0.0).astype(f32)
-    proj_out[...] = dot_t(eye, proj, precise)
-
-    mixing = spread(((inv_one, 0), (-dot(inv_one, proj, precise), block)), width)
-
-    def mix_step(i, total):
-        q = fold_rows(dot(mixing, stack[i]), m)
-        both = jnp.concatenate(pieces(q), axis=0).astype(b16)
-        ortho[i] = both
-        return total + dot_t(both, both)
-
-    second = lax.fori_loop(0, nf * nx, mix_step, jnp.zeros((block, block), f32), unroll=4)
-    tile[0:m, 0:block] = fold_rows(second, m) * inv_cells
-    tile[0:m, block:width] = jnp.zeros((m, width - block), f32)
+    proj_out[...] = proj
+
+    depth = stack.shape[1]
+
+    def pick_own(level):
+        row, col = iota((m, depth), 0), iota((m, depth), 1)
+        return where01((col % m == row) & (col < (3 - level) * 2 * m))
+
+    def pick_prior(level):
+        row, col = iota((k, depth), 0), iota((k, depth), 1)
+        at = (col + (pad_k - own3 % pad_k)) % pad_k
+        return where01((at % k == row) & (at < (3 - level) * k) & (col >= own3))
+
+    col = iota((m, depth), 1)
+    group = jnp.where(col < own3, (col // m) % 2, jnp.where(col < own3 + pad_k, 0, 1))
+    mixing = spread(
+        ((inv_one, pick_own), (-dot(inv_one, proj, precise), pick_prior)), 3, 2, group
+    )
+
+    def mix_step(step, total):
+        for half in range(2):
+            q = jnp.concatenate(
+                [
+                    fold_rows(dot(mixing, stack[4 * step + 2 * half + j]), 2 * m)
+                    for j in range(2)
+                ],
+                axis=0,
+            )
+            both = jnp.concatenate(pieces(q)[:2], axis=0).astype(b16)
+            ortho[step, half * 8 * m : (half + 1) * 8 * m, :] = both
+            total = total + dot_t(both, both)
+        return total
+
+    second = lax.fori_loop(
+        0, steps // 8, mix_step, jnp.zeros((8 * m, 8 * m), f32), unroll=2
+    )
+    second = fold_rows(second, 4 * m)
+    col = iota(second.shape, 1)
+    second = jnp.where((col // m) % 4 == iota(second.shape, 0) // m, second, 0.0)
     sums = all_reduce(
-        tile[0:m, :], (("gy", gy, py, y2, y2s, y2r), ("gx", gx, px, x2, x2s, x2r))
-    )
-    upper_two, inv_two = factor(dot_t(sums, selector(m, width, 0, 3), precise))
+        fold_rows(second, m) * inv_cells,
+        (("gy", gy, py, y2, y2s, y2r), ("gx", gx, px, x2, x2s, x2r)),
+    )
+    pick_m = where01(iota(sums.shape, 1) % m == iota(sums.shape, 0))
+    upper_two, inv_two = factor(dot_t(sums, pick_m, precise))
     tri_out[...] = dot(upper_two, upper_one, precise)
-    last = spread(((inv_two, 0),), block)
-
-    def last_step(i, carry):
-        x, f = i // nf, i % nf
-        q = fold_rows(dot(last, ortho[i]), m)
-        for h in range(halves):
-            out[lines(f, x, h, m), :] = q[:, h * 128 : (h + 1) * 128]
+
+    def pick_two(level):
+        row, col = iota((m, 16 * m), 0), iota((m, 16 * m), 1)
+        return where01((col % m == row) & ((col // (4 * m)) % 2 < 2 - level))
+
+    col = iota((m, 16 * m), 1)
+    last = spread(((inv_two, pick_two),), 2, 8, (col // (8 * m)) * 4 + (col // m) % 4)
+
+    def last_step(step, carry):
+        q = fold_rows(dot(last, ortho[step]), 8 * m)
+        for g in range(8):
+            i = 8 * step + g
+            x, f = i // nf, i % nf
+            for h in range(halves):
+                out[lines(f, x, h, m), :] = q[g * m : (g + 1) * m, h * 128 : (h + 1) * 128]
         return carry
 
-    lax.fori_loop(0, nf * nx, last_step, 0, unroll=4)
+    lax.fori_loop(0, steps // 8, last_step, 0, unroll=2)
 
     pl.when(gx < px - 1)(send_up.wait_send)
     pl.when(gx > 0)(send_down.wait_send)
@@ -339,8 +402,8 @@
     k, types = prior_basis.shape[0], wall_table.shape[0]
     px, py = lax.axis_size("gx"), lax.axis_size("gy")
     inv_cells = 1.0 / (nf * nx * px * ny * py)
-    block = 3 * m
-    width = block + -(-3 * k // 16) * 16
+    depth = 6 * m + 2 * (-(-3 * k // 16) * 16)
+    steps, width = nf * nx, 8 * m
     rows, halves = nf * m, ny // 128
     hbm = pl.BlockSpec(memory_space=pl.ANY)
     vmem = pl.BlockSpec(memory_space=pltpu.VMEM)
@@ -350,7 +413,7 @@
         functools.partial(kernel, (m, k, nf, nx, ny, types), inv_cells),
         out_shape=(
             jax.ShapeDtypeStruct((halves * m * nf * nx, 128), f32),
-            jax.ShapeDtypeStruct((k, m), f32),
+            jax.ShapeDtypeStruct((m, k), f32),
             jax.ShapeDtypeStruct((m, m), f32),
         ),
         in_specs=[hbm, hbm, vmem, vmem, vmem, smem, smem, vmem, vmem],
@@ -361,12 +424,14 @@
             pltpu.VMEM((nx + 4, rows, ny), f32),
             pltpu.VMEM((nx, rows, 128), f32),
             pltpu.VMEM((nx, rows, 128), f32),
-            pltpu.VMEM((rows, ny), f32),
+            pltpu.VMEM((2, rows, ny), f32),
+            pltpu.VMEM((2, rows, ny), f32),
+            pltpu.VMEM((nx, rows, ny), f32),
             pltpu.VMEM((2, 2, rows, ny), b16),
             pltpu.VMEM((2, rows, rows), b16),
             pltpu.VMEM((2, rows, rows), b16),
-            pltpu.VMEM((nf * nx, width, ny), b16),
-            pltpu.VMEM((nf * nx, block, ny), b16),
+            pltpu.VMEM((steps // 2, depth, ny), b16),
+            pltpu.VMEM((steps // 8, 16 * m, ny), b16),
             pltpu.VMEM((m + k, width), f32),
             pltpu.VMEM((py, m + k, width), f32),
             pltpu.VMEM((px, m + k, width), f32),
@@ -384,7 +449,7 @@
         field_rates, wall_table, wall_mask, wall_type,
     )
     new = new.reshape(m, nf, halves, nx, 128).transpose(0, 1, 3, 2, 4).reshape(m, nf, nx, ny)
-    return (new, proj, tri)
+    return (new, proj.T, tri)
 
 
 def solution(mesh):

time: 129 us -> 98.4 us (0.76)
  Pallas kernels: 123 us -> 92.3 us
    pallas_call x1, Pallas kernels: 123 us -> 92.3 us  [on_device(): pl.pallas_call(functools.partial(kernel, (m, k, nf, nx, ny, types), inv_c...]
    unnamed x5 -> x7, local copies, waits for them, and re-layouts: 5.97 us -> 5.19 us
where the time goes in v1:
time: 98.4 us; the launch traced here: 98.1 us
  Pallas kernels  92.3 us (94%)
  local copies, waits for them, and re-layouts  5.19 us (5%)
    pallas_call x1, Pallas kernels, on_device(): pl.pallas_call(functools.partial(kernel, (m, k, nf, nx, ny, types), inv_c...  92.3 us
    unnamed x7, local copies, waits for them, and re-layouts  5.19 us

profile of v1, /device:TPU:0, one launch (start us, length us, event | category | flops | bytes accessed | tf_op | source)
XLA Modules:
  0.0 98.1 jit_solution(12332403982003689717)
XLA Ops:
  0.6 92.3 %shard_map.112 = (f32[6656,128]{1,0:T(8,128)}, f32[16,24]{1,0:T(8,128)}, f32[16,16]{1,0:T(8,128)}) custom-call(f32[6656,128]{1,0:T(8,128)} %bitcast.17, f32[9984,128]{1,0:T(8,128)} %bitcast.16, f32[26,26]{1,0:T(8,128)} %along.1, f32[26,26]{1,0:T(8,128)} %across.1, f32[8,256]{1,0:T(8,128)} %coll.1, f32[26]{0:T(128)} %rates.1, f32[4,26]{1,0:T(4,128)} %table.1, ...), custom_call_target="tpu_custom_call" | custom-call | tf_op jit(solution)/shard_map/pallas_call | solution.py:412
  92.9 0.0 copy-start.1
  92.9 0.0 copy-start
  92.9 4.0 %copy.15 = f32[16,26,8,256]{3,2,1,0:T(8,128)} copy(f32[16,26,8,256]{3,2,1,0:T(8,128)} %bitcast.18) | data formatting | bytes 6815744
  96.9 0.0 copy-done.1
  96.9 0.6 copy.16
  97.5 0.0 copy-done
  97.5 0.6 copy.17
Async XLA Ops:
  92.9 4.0 %copy-start.1 = (f32[16,24]{1,0:T(8,128)S(1)}, f32[16,24]{1,0:T(8,128)}, u32[]{:S(2)}) copy-start(f32[16,24]{1,0:T(8,128)} %get-tuple-element.7) | copy-start | bytes 4612
  92.9 4.6 %copy-start = (f32[16,16]{1,0:T(8,128)S(1)}, f32[16,16]{1,0:T(8,128)}, u32[]{:S(2)}) copy-start(f32[16,16]{1,0:T(8,128)} %get-tuple-element.14) | copy-start | bytes 3076

commit v2 on v1

--- a/solution.py
+++ b/solution.py
@@ -116,7 +116,7 @@
                 vals[x + 2, pl.ds(at, m), lanes] = kv[lines(f, x, h, m), :]
             return carry
 
-        lax.fori_loop(0, nf, body, 0, unroll=2)
+        lax.fori_loop(0, nf, body, 0, unroll=nf // 2)
 
     def remote(src, dst, index, where):
         return pltpu.make_async_remote_copy(
@@ -225,7 +225,7 @@
                 grad[index, 1, at, :] = (g - high.astype(f32)).astype(b16)
             return carry
 
-        lax.fori_loop(0, nf, body, 0, unroll=2)
+        lax.fori_loop(0, nf, body, 0, unroll=nf // 2)
         for index in range(2):
             high, low = grad[index, 0], grad[index, 1]
             app[x] += dot(kron_h[index], high) + dot(kron_h[index], low) + dot(kron_l[index], high)
@@ -264,7 +264,7 @@
             grad[0, 1, at, :] = (g - high.astype(f32)).astype(b16)
             return carry
 
-        lax.fori_loop(0, nf, body, 0, unroll=2)
+        lax.fori_loop(0, nf, body, 0, unroll=nf // 2)
         high, low = grad[0, 0], grad[0, 1]
         app[x_near] += dot(kron_h[0], high) + dot(kron_h[0], low) + dot(kron_l[0], high)
 

time: 98.4 us -> 91.6 us (0.931)
  Pallas kernels: 92.3 us -> 85.5 us
    pallas_call x1, Pallas kernels: 92.3 us -> 85.5 us  [on_device(): pl.pallas_call(functools.partial(kernel, (m, k, nf, nx, ny, types), inv_c...]
where the time goes in v2:
time: 91.6 us; the launch traced here: 91.4 us
  Pallas kernels  85.5 us (93%)
  local copies, waits for them, and re-layouts  5.19 us (6%)
    pallas_call x1, Pallas kernels, on_device(): pl.pallas_call(functools.partial(kernel, (m, k, nf, nx, ny, types), inv_c...  85.5 us
    unnamed x7, local copies, waits for them, and re-layouts  5.19 us

profile of v2, /device:TPU:0, one launch (start us, length us, event | category | flops | bytes accessed | tf_op | source)
XLA Modules:
  0.0 91.4 jit_solution(5649307087974446554)
XLA Ops:
  0.6 85.5 %shard_map.112 = (f32[6656,128]{1,0:T(8,128)}, f32[16,24]{1,0:T(8,128)}, f32[16,16]{1,0:T(8,128)}) custom-call(f32[6656,128]{1,0:T(8,128)} %bitcast.17, f32[9984,128]{1,0:T(8,128)} %bitcast.16, f32[26,26]{1,0:T(8,128)} %along.1, f32[26,26]{1,0:T(8,128)} %across.1, f32[8,256]{1,0:T(8,128)} %coll.1, f32[26]{0:T(128)} %rates.1, f32[4,26]{1,0:T(4,128)} %table.1, ...), custom_call_target="tpu_custom_call" | custom-call | tf_op jit(solution)/shard_map/pallas_call | solution.py:412
  86.2 0.0 copy-start.1
  86.2 0.0 copy-start
  86.2 4.0 %copy.15 = f32[16,26,8,256]{3,2,1,0:T(8,128)} copy(f32[16,26,8,256]{3,2,1,0:T(8,128)} %bitcast.18) | data formatting | bytes 6815744
  90.2 0.0 copy-done.1
  90.2 0.6 copy.16
  90.8 0.0 copy-done
  90.8 0.6 copy.17
Async XLA Ops:
  86.2 4.0 %copy-start.1 = (f32[16,24]{1,0:T(8,128)S(1)}, f32[16,24]{1,0:T(8,128)}, u32[]{:S(2)}) copy-start(f32[16,24]{1,0:T(8,128)} %get-tuple-element.7) | copy-start | bytes 4612
  86.2 4.6 %copy-start = (f32[16,16]{1,0:T(8,128)S(1)}, f32[16,16]{1,0:T(8,128)}, u32[]{:S(2)}) copy-start(f32[16,16]{1,0:T(8,128)} %get-tuple-element.14) | copy-start | bytes 3076
